TPU v7x, 128 devices: a whole 4x4x4 slice. The times are simulated.
128 devices in a mesh: ctx: 8 (over x_lo, y), grp: 8 (over z, core), head: 2 (over x_hi).
Axes of the slice: x: 4 (x_hi: 2, x_lo: 2; x = x_hi * 2 + x_lo), y: 4, z: 4, core: 2. Of those that a mesh axis runs over, the one named last changes fastest.
Arguments:
- prefill_query: bfloat16 [8192, 8192], P(('ctx', 'grp'), 'head'), may hold values from -400 to 400
- prefill_kv: bfloat16 [8192, 2048], P(('ctx', 'grp'), 'head'), may hold values from -6 to 6
- page_dest: int32 [256, 1], P(('ctx', 'grp')), may hold values from 0 to 7; in each aligned block of 4 rows (0 to 3, 4 to 7, ...) at most 2 rows name the same one
- cache_pool: bfloat16 [8, 8, 128, 32, 2048], P('ctx', 'grp', None, None, 'head'), may hold values from -6 to 6
- page_table: int32 [256, 32], P('grp', 'ctx'), may hold values from 0 to 127, as said below
- context_len: int32 [256], P('grp'), may hold values from 1 to 1024
- dec_query: bfloat16 [4, 256, 8192], P(None, 'grp', 'head'), may hold values from -400 to 400
- dec_new: bfloat16 [4, 256, 2048], P(None, 'grp', 'head'), may hold values from -6 to 6
Outputs:
- prefill_out: bfloat16 [8192, 8192], P(('ctx', 'grp'), 'head')
- arrivals: bfloat16 [8, 8, 16, 32, 2048], P('grp', 'ctx', None, None, 'head')
- dec_out: bfloat16 [4, 256, 8192], P(None, 'grp', 'head')
Inputs may be any that keep to these rules, and one draw needn't show every extreme that they name: `page_dest`: the 4 pages of one index of ctx and grp name one decode group at most 2 times. `page_table`: for each decode group and index c of ctx, the entries of columns c * 4 to (c+1) * 4 - 1 over that group's 32 requests name each of its 128 pool pages once.
All inputs are finite; a program needn't handle non-finite values.
Results may differ from a plain program's by a relative error of at most 0.015.
Values may be sent and summed in bfloat16 or wider, within the bound.
A program may use at most 128 MiB of HBM per device.

v0:
```python
import jax
import jax.numpy as jnp
from jax import lax
from jax.sharding import PartitionSpec as P

QH = 64
KVH = 8
HD = 128
PAGE = 32


NEG = -1e30


def page_ranks(dest):
    count = dest.shape[0]
    earlier = jnp.arange(count)[None, :] < jnp.arange(count)[:, None]
    same = dest[:, None] == dest[None, :]
    return jnp.sum(jnp.logical_and(same, earlier), axis=1)


def on_device(
    prefill_query, prefill_kv, page_dest, cache_pool, page_table, context_len, dec_query, dec_new
):
    scale = HD ** (-0.5)
    tok = prefill_query.shape[0]
    kvh = prefill_kv.shape[1] // (2 * HD)
    group = QH // KVH
    feat = kvh * 2 * HD
    query = prefill_query.reshape(tok, kvh, group, HD)
    q_start = lax.axis_index(("ctx", "grp")) * tok
    q_pos = q_start + jnp.arange(tok)

    def one_block(carry, piece, start):
        run_max, run_sum, run_acc = carry
        rows = piece.shape[0]
        pair = piece.reshape(rows, kvh, 2, HD)
        score = (
            jnp.einsum("ikgd,jkd->kgij", query, pair[:, :, 0], preferred_element_type=jnp.float32)
            * scale
        )
        allowed = (start + jnp.arange(rows))[None, :] <= q_pos[:, None]
        masked = jnp.where(allowed[None, None], score, NEG)
        new_max = jnp.maximum(run_max, jnp.max(masked, axis=-1))
        expo = jnp.where(allowed[None, None], jnp.exp(masked - new_max[..., None]), 0.0)
        fix = jnp.exp(run_max - new_max)
        weight = expo.astype(jnp.bfloat16)
        run_sum = run_sum * fix + jnp.sum(expo, axis=-1)
        run_acc = run_acc * fix[..., None] + jnp.einsum(
            "kgij,jkd->kgid", weight, pair[:, :, 1], preferred_element_type=jnp.float32
        )
        return (new_max, run_sum, run_acc)

    init = (
        jnp.full((kvh, group, tok), NEG, jnp.float32),
        jnp.zeros((kvh, group, tok), jnp.float32),
        jnp.zeros((kvh, group, tok, HD), jnp.float32),
    )
    carry = init
    piece = lax.all_gather(prefill_kv, ("ctx", "grp"), axis=0, tiled=True)
    rows = piece.shape[0]
    width = 512
    blocks = piece.reshape(rows // width, width, feat)
    offsets = jnp.arange(rows // width, dtype=jnp.int32) * width

    def advance(held, item):
        return (one_block(held, item[0], item[1]), None)

    carry, unused = lax.scan(advance, carry, (blocks, offsets))
    run_max, run_sum, run_acc = carry
    prefill_out = (
        jnp.transpose(run_acc / run_sum[..., None], (2, 0, 1, 3))
        .reshape(tok, kvh * group * HD)
        .astype(jnp.bfloat16)
    )
    npages = tok // PAGE
    ngrp = lax.axis_size("grp")
    cap = max(2, 2 * npages // ngrp)
    slots = ngrp * cap
    pages = prefill_kv.reshape(npages, PAGE * feat)
    dest = page_dest[:, 0]
    every_pages, every_dest = (
        lax.all_gather(pages, "grp", axis=0, tiled=True),
        lax.all_gather(dest, "grp", axis=0, tiled=True),
    )
    dest_rows = every_dest.reshape(ngrp, npages)
    rank_rows = jax.vmap(page_ranks)(dest_rows)
    source = jnp.arange(ngrp)[:, None]
    slot_ids = jnp.where(dest_rows == lax.axis_index("grp"), source * cap + rank_rows, -1).reshape(
        -1
    )
    pick = (jnp.arange(slots)[:, None] == slot_ids[None, :]).astype(jnp.bfloat16)
    arrivals = (
        jnp.dot(pick, every_pages, preferred_element_type=jnp.float32)
        .astype(jnp.bfloat16)
        .reshape(1, 1, slots, PAGE, feat)
    )
    steps = dec_query.shape[0]
    req = dec_query.shape[1]
    maxp = page_table.shape[1]
    span = maxp * PAGE
    ctx_index = lax.axis_index("ctx")
    dquery = dec_query.reshape(steps, req, kvh, group, HD)
    cached = cache_pool[0, 0][page_table].reshape(req, span, kvh, 2, HD)
    newkv = dec_new.reshape(steps, req, kvh, 2, HD)
    s_old = (
        jnp.einsum(
            "trkgd,rjkd->trkgj", dquery, cached[:, :, :, 0], preferred_element_type=jnp.float32
        )
        * scale
    )
    s_new = (
        jnp.einsum(
            "trkgd,urkd->trkgu", dquery, newkv[:, :, :, 0], preferred_element_type=jnp.float32
        )
        * scale
    )
    valid = (ctx_index * span + jnp.arange(span))[None, :] < context_len[:, None]
    new_ok = jnp.logical_and(
        jnp.arange(steps)[None, :] <= jnp.arange(steps)[:, None], ctx_index == 0
    )
    mask_old = valid[None, :, None, None, :]
    mask_new = new_ok[:, None, None, None, :]
    masked_old = jnp.where(mask_old, s_old, NEG)
    masked_new = jnp.where(mask_new, s_new, NEG)
    top = jnp.maximum(jnp.max(masked_old, axis=-1), jnp.max(masked_new, axis=-1))
    e_old = jnp.where(mask_old, jnp.exp(masked_old - top[..., None]), 0.0)
    e_new = jnp.where(mask_new, jnp.exp(masked_new - top[..., None]), 0.0)
    total = jnp.sum(e_old, axis=-1) + jnp.sum(e_new, axis=-1)
    summed = jnp.einsum(
        "trkgj,rjkd->trkgd",
        e_old.astype(jnp.bfloat16),
        cached[:, :, :, 1],
        preferred_element_type=jnp.float32,
    )
    summed = summed + jnp.einsum(
        "trkgu,urkd->trkgd",
        e_new.astype(jnp.bfloat16),
        newkv[:, :, :, 1],
        preferred_element_type=jnp.float32,
    )
    top_all = lax.pmax(top, "ctx")
    fix = jnp.exp(top - top_all)
    total_all, summed_all = (
        lax.psum((total * fix).astype(jnp.bfloat16), "ctx").astype(jnp.float32),
        lax.psum((summed * fix[..., None]).astype(jnp.bfloat16), "ctx").astype(jnp.float32),
    )
    dec_out = (
        (summed_all / total_all[..., None])
        .reshape(steps, req, kvh * group * HD)
        .astype(jnp.bfloat16)
    )
    return (prefill_out, arrivals, dec_out)


def solution(mesh):
    placed = (
        P(("ctx", "grp"), "head"),
        P(("ctx", "grp"), "head"),
        P(("ctx", "grp"), None),
        P("ctx", "grp", None, None, "head"),
        P("grp", "ctx"),
        P("grp"),
        P(None, "grp", "head"),
        P(None, "grp", "head"),
    )
    return jax.shard_map(
        on_device,
        mesh=mesh,
        in_specs=placed,
        out_specs=(
            P(("ctx", "grp"), "head"),
            P("grp", "ctx", None, None, "head"),
            P(None, "grp", "head"),
        ),
        check_vma=False,
    )
```

profile of v0, /device:TPU:1, one launch (start us, length us, event | category | flops | bytes accessed | tf_op | source)
XLA Modules:
  0.0 581.1 jit_solution(8628363270036438690)
XLA Ops:
  11.1 9.9 %gather_fusion = bf16[128,32,1024]{2,1,0:T(8,128)(2,1)} fusion(bf16[128,32,1024]{2,1,0:T(8,128)(2,1)} %bitcast.127, s32[1024]{0:T(1024)S(1)} %pad_clamp_fusion), kind=kCustom, calls=%fused_computation | custom fusion | bytes 16777728 | tf_op jit(solution)/shard_map/gather | solution.py:104
  21.0 14.3 %reshape.153 = bf16[32,128,4,2,128]{4,3,2,1,0:T(2,128)(2,1)} reshape(bf16[128,32,1024]{2,1,0:T(8,128)(2,1)} %gather_fusion) | data formatting | bytes 16777216 | tf_op jit(solution)/shard_map/reshape | solution.py:104
  35.3 17.0 %fusion.49 = (bf16[32,128,4,1,128]{4,3,2,1,0:T(2,128)(2,1)}, bf16[32,128,4,1,128]{4,3,2,1,0:T(2,128)(2,1)S(1)}) fusion(bf16[32,128,4,2,128]{4,3,2,1,0:T(2,128)(2,1)} %reshape.153), kind=kLoop, calls=%fused_computation.85 | loop fusion | bytes 16777216 | tf_op jit(solution)/shard_map/slice | solution.py:133
  52.3 4.8 fusion.51
  60.8 32.0 %pmax.7 = f32[4,32,4,8]{3,0,2,1:T(4,128)} all-reduce(f32[4,32,4,8]{3,0,2,1:T(4,128)S(1)} %max.12), channel_id=1, replica_groups=mesh['ctx'=8,'grp'=8,'head'=2] {'ctx'}, use_global_device_ids=true, to_apply=%region_7.8 | all-reduce | flops 4096 | bytes 32768 | tf_op jit(solution)/shard_map/pmax | solution.py:142
  97.2 5.6 fusion.19
  107.1 16.2 %all-reduce = s32[32]{0:T(128)S(1)} all-reduce(s32[32]{0:T(128)S(1)} %bitcast_dynamic-update-slice_fusion), channel_id=2, replica_groups=mesh['ctx'=8,'grp'=8,'head'=2] {'grp'}, use_global_device_ids=true, to_apply=%add | all-reduce | flops 32 | bytes 256
  123.8 26.6 %psum.15 = bf16[4,32,4,8]{3,0,2,1:T(4,128)(2,1)S(1)} all-reduce(bf16[4,32,4,8]{3,0,2,1:T(4,128)(2,1)S(1)} %get-tuple-element.128), channel_id=1, replica_groups=mesh['ctx'=8,'grp'=8,'head'=2] {'ctx'}, use_global_device_ids=true, to_apply=%region_11.12 | all-reduce | flops 4096 | bytes 16384 | tf_op jit(solution)/shard_map/psum | solution.py:145
  150.5 40.7 %all-reduce.3.cloned.1.call-done = bf16[4,32,4,8,128]{4,3,0,2,1:T(8,128)(2,1)} async-done(((bf16[4,32,4,8,128]{4,3,0,2,1:T(8,128)(2,1)}), bf16[4,32,4,8,128]{4,3,0,2,1:T(8,128)(2,1)}) %all-reduce.3.cloned.1.call-update) | async-done | bytes 1048592 | tf_op jit(solution)/shard_map/psum | solution.py:146
  198.9 69.5 %all-gather.5.cloned.1.call-done = bf16[8192,1024]{1,0:T(8,128)(2,1)} async-done(((bf16[128,1024]{1,0:T(8,128)(2,1)}), bf16[8192,1024]{1,0:T(8,128)(2,1)}) %all-gather.5.cloned.1.call-update) | async-done | bytes 16777232 | tf_op jit(solution)/shard_map/all_gather | solution.py:60
  268.5 301.1 %while.15 = (s32[]{:T(128)}, f32[4,8,128]{2,1,0:T(8,128)S(1)}, f32[4,8,128]{2,1,0:T(8,128)S(1)}, f32[4,8,128,128]{3,2,1,0:T(8,128)}, s32[16]{0:T(128)S(1)}, /*in...) while((s32[]{:T(128)}, f32[4,8,128]{2,1,0:T(8,128)S(1)}, ...), condition=%wide.region_3.4_spmd.clone, body=%wide.region_0.3_spmd.clone.sunk | while | flops 1102664320 | bytes 69735600 | solution.py:69
  276.3 4.7 fusion.63
  294.0 4.7 fusion.63
  299.8 5.2 fusion.65
  312.8 4.7 fusion.63
  318.7 5.2 fusion.65
  331.7 4.7 fusion.63
  337.6 5.2 fusion.65
  350.6 4.7 fusion.63
  356.5 5.2 fusion.65
  375.4 5.2 fusion.65
  394.3 5.2 fusion.65
  407.3 4.7 fusion.63
  413.2 5.2 fusion.65
  432.1 5.2 fusion.65
  451.0 5.2 fusion.65
  469.9 5.2 fusion.65
  488.8 5.2 fusion.65
  507.7 5.2 fusion.65
  526.6 5.2 fusion.65
  545.4 5.2 fusion.65
  564.3 5.2 fusion.65
  (273 shorter events, 220.7 us)
Async XLA Ops:
  8.0 1.6 copy-start.5
  8.0 2.8 copy-start.6
  8.0 183.1 %all-reduce.3.cloned.1.call-start = ((), (), s32[]{:S(2)}) async-start(), calls=%async_computation.1 | async-start | bytes 2097152 | tf_op jit(solution)/shard_map/psum | solution.py:146
  9.6 42.8 %copy-start.2 = (bf16[16,8,32,128]{3,2,1,0:T(8,128)(2,1)}, bf16[16,8,32,128]{3,2,1,0:T(8,128)(2,1)S(1)}, u32[]{:S(2)}) copy-start(bf16[16,8,32,128]{3,2,1,0:T(8,128)(2,1)S(1)} %copy.94) | copy-start | bytes 3145732
  35.3 17.0 %copy-start.7 = (s32[32]{0:T(128)S(1)}, s32[32]{0:T(128)}, u32[]{:S(2)}) copy-start(s32[32]{0:T(128)} %param.15) | copy-start | bytes 388
  95.6 1.4 copy-start.4
  97.2 5.6 copy-start.3
  102.8 1.6 copy-start.1
  102.8 91.6 %all-gather.7.cloned.1.call-start = ((), (), s32[]{:S(2)}) async-start(), calls=%async_computation.2 | async-start | bytes 2359296 | tf_op jit(solution)/shard_map/all_gather | solution.py:83
  103.8 164.7 %all-gather.5.cloned.1.call-start = ((), (), s32[]{:S(2)}) async-start(), calls=%async_computation | async-start | bytes 17039360 | tf_op jit(solution)/shard_map/all_gather | solution.py:60
  104.4 1.4 copy-start.9
  104.4 2.6 copy-start.8
  276.3 5.8 %copy-start = (f32[4,512,128,8]{2,1,3,0:T(8,128)S(1)}, f32[4,512,128,8]{2,1,3,0:T(8,128)}, u32[]{:S(2)}) copy-start(f32[4,512,128,8]{2,1,3,0:T(8,128)} %get-tuple-element.194) | copy-start | bytes 25165828 | tf_op jit(solution)/shard_map/while
  293.9 5.8 %copy-start = (f32[4,512,128,8]{2,1,3,0:T(8,128)S(1)}, f32[4,512,128,8]{2,1,3,0:T(8,128)}, u32[]{:S(2)}) copy-start(f32[4,512,128,8]{2,1,3,0:T(8,128)} %get-tuple-element.194) | copy-start | bytes 25165828 | tf_op jit(solution)/shard_map/while
  312.8 5.8 %copy-start = (f32[4,512,128,8]{2,1,3,0:T(8,128)S(1)}, f32[4,512,128,8]{2,1,3,0:T(8,128)}, u32[]{:S(2)}) copy-start(f32[4,512,128,8]{2,1,3,0:T(8,128)} %get-tuple-element.194) | copy-start | bytes 25165828 | tf_op jit(solution)/shard_map/while
  331.7 5.8 %copy-start = (f32[4,512,128,8]{2,1,3,0:T(8,128)S(1)}, f32[4,512,128,8]{2,1,3,0:T(8,128)}, u32[]{:S(2)}) copy-start(f32[4,512,128,8]{2,1,3,0:T(8,128)} %get-tuple-element.194) | copy-start | bytes 25165828 | tf_op jit(solution)/shard_map/while
  350.6 5.8 %copy-start = (f32[4,512,128,8]{2,1,3,0:T(8,128)S(1)}, f32[4,512,128,8]{2,1,3,0:T(8,128)}, u32[]{:S(2)}) copy-start(f32[4,512,128,8]{2,1,3,0:T(8,128)} %get-tuple-element.194) | copy-start | bytes 25165828 | tf_op jit(solution)/shard_map/while
  369.5 5.8 %copy-start = (f32[4,512,128,8]{2,1,3,0:T(8,128)S(1)}, f32[4,512,128,8]{2,1,3,0:T(8,128)}, u32[]{:S(2)}) copy-start(f32[4,512,128,8]{2,1,3,0:T(8,128)} %get-tuple-element.194) | copy-start | bytes 25165828 | tf_op jit(solution)/shard_map/while
  388.4 5.8 %copy-start = (f32[4,512,128,8]{2,1,3,0:T(8,128)S(1)}, f32[4,512,128,8]{2,1,3,0:T(8,128)}, u32[]{:S(2)}) copy-start(f32[4,512,128,8]{2,1,3,0:T(8,128)} %get-tuple-element.194) | copy-start | bytes 25165828 | tf_op jit(solution)/shard_map/while
  407.3 5.8 %copy-start = (f32[4,512,128,8]{2,1,3,0:T(8,128)S(1)}, f32[4,512,128,8]{2,1,3,0:T(8,128)}, u32[]{:S(2)}) copy-start(f32[4,512,128,8]{2,1,3,0:T(8,128)} %get-tuple-element.194) | copy-start | bytes 25165828 | tf_op jit(solution)/shard_map/while
  426.2 5.8 %copy-start = (f32[4,512,128,8]{2,1,3,0:T(8,128)S(1)}, f32[4,512,128,8]{2,1,3,0:T(8,128)}, u32[]{:S(2)}) copy-start(f32[4,512,128,8]{2,1,3,0:T(8,128)} %get-tuple-element.194) | copy-start | bytes 25165828 | tf_op jit(solution)/shard_map/while
  445.1 5.8 %copy-start = (f32[4,512,128,8]{2,1,3,0:T(8,128)S(1)}, f32[4,512,128,8]{2,1,3,0:T(8,128)}, u32[]{:S(2)}) copy-start(f32[4,512,128,8]{2,1,3,0:T(8,128)} %get-tuple-element.194) | copy-start | bytes 25165828 | tf_op jit(solution)/shard_map/while
  464.0 5.8 %copy-start = (f32[4,512,128,8]{2,1,3,0:T(8,128)S(1)}, f32[4,512,128,8]{2,1,3,0:T(8,128)}, u32[]{:S(2)}) copy-start(f32[4,512,128,8]{2,1,3,0:T(8,128)} %get-tuple-element.194) | copy-start | bytes 25165828 | tf_op jit(solution)/shard_map/while
  482.9 5.8 %copy-start = (f32[4,512,128,8]{2,1,3,0:T(8,128)S(1)}, f32[4,512,128,8]{2,1,3,0:T(8,128)}, u32[]{:S(2)}) copy-start(f32[4,512,128,8]{2,1,3,0:T(8,128)} %get-tuple-element.194) | copy-start | bytes 25165828 | tf_op jit(solution)/shard_map/while
  501.8 5.8 %copy-start = (f32[4,512,128,8]{2,1,3,0:T(8,128)S(1)}, f32[4,512,128,8]{2,1,3,0:T(8,128)}, u32[]{:S(2)}) copy-start(f32[4,512,128,8]{2,1,3,0:T(8,128)} %get-tuple-element.194) | copy-start | bytes 25165828 | tf_op jit(solution)/shard_map/while
  520.7 5.8 %copy-start = (f32[4,512,128,8]{2,1,3,0:T(8,128)S(1)}, f32[4,512,128,8]{2,1,3,0:T(8,128)}, u32[]{:S(2)}) copy-start(f32[4,512,128,8]{2,1,3,0:T(8,128)} %get-tuple-element.194) | copy-start | bytes 25165828 | tf_op jit(solution)/shard_map/while
  539.6 5.8 %copy-start = (f32[4,512,128,8]{2,1,3,0:T(8,128)S(1)}, f32[4,512,128,8]{2,1,3,0:T(8,128)}, u32[]{:S(2)}) copy-start(f32[4,512,128,8]{2,1,3,0:T(8,128)} %get-tuple-element.194) | copy-start | bytes 25165828 | tf_op jit(solution)/shard_map/while
  558.5 5.8 %copy-start = (f32[4,512,128,8]{2,1,3,0:T(8,128)S(1)}, f32[4,512,128,8]{2,1,3,0:T(8,128)}, u32[]{:S(2)}) copy-start(f32[4,512,128,8]{2,1,3,0:T(8,128)} %get-tuple-element.194) | copy-start | bytes 25165828 | tf_op jit(solution)/shard_map/while
Sparse Core Ops, SparseCore 0:
  102.9 88.1 all-reduce.2
Sparse Core Ops, SparseCore 1:
  105.6 32.7 all-gather.6
  139.9 128.5 all-gather.4
where the time goes:
time: 583 us; the launch traced here: 581 us
  matrix products  173 us (30%)
  local copies, waits for them, and re-layouts  112 us (19%)
  waiting for transfers between devices  111 us (19%)
  other arithmetic  92.8 us (16%)
  blocking collectives  74.8 us (13%)
  between operations  16.5 us (3%)
    dot_general x16, matrix products, one_block(): jnp.einsum('kgij,jkd->kgid', weight, pair[:, :, 1], preferred_element_typ...  82.6 us
    reduce_sum x16, other arithmetic, one_block(): run_sum = run_sum * fix + jnp.sum(expo, axis=-1)  74.7 us
    dot_general x16, matrix products, one_block(): jnp.einsum('ikgd,jkd->kgij', query, pair[:, :, 0], preferred_element_type...  74.6 us
    all_gather x1, waiting for transfers between devices, on_device(): piece = lax.all_gather(prefill_kv, ('ctx', 'grp'), axis=0, tiled=True)  69.5 us
    psum x1, waiting for transfers between devices, on_device(): lax.psum((summed * fix[..., None]).astype(jnp.bfloat16), 'ctx')  40.7 us
    dynamic_slice x48, local copies, waits for them, and re-layouts, on_device(): carry, unused = lax.scan(advance, carry, (blocks, offsets))  38.7 us
    pmax x1, blocking collectives, on_device(): top_all = lax.pmax(top, 'ctx')  32 us
    psum x1, blocking collectives, on_device(): lax.psum((total * fix).astype(jnp.bfloat16), 'ctx').astype(jnp.float32)  26.6 us
  transfers between devices with their start and end apart: 3, of which 2 were waited for; matrix products, arithmetic and copies ran while one was open for 2% of the time, Pallas kernels for 0%

commit v1 on v0

v1 whole, which is shorter than its diff:
```python
import jax
import jax.numpy as jnp
from jax import lax
from jax.experimental import pallas as pl
from jax.experimental.pallas import tpu as pltpu
from jax.sharding import PartitionSpec as P

HD = 128
NEG = -1e30
SCALE = HD**-0.5
EXP2 = SCALE * 1.4426950408889634
MESH = pl.DeviceIdType.MESH
CHAIN = 256


def softmax_step(s, v, state):
    m, l, acc = state
    mn = jnp.maximum(m, jnp.max(s, axis=1, keepdims=True))
    al = jnp.exp2((m - mn) * EXP2)
    p = jnp.exp2((s - mn) * EXP2)
    part = p[:, 0:HD]
    for t in range(1, s.shape[1] // HD):
        part = part + p[:, t * HD : (t + 1) * HD]
    acc = acc * al + jnp.dot(p.astype(jnp.bfloat16), v, preferred_element_type=jnp.float32)
    return mn, l * al + part, acc


def flash_chunk(qs, k, v, states, allowed):
    def score(q):
        s = lax.dot_general(q, k, (((1,), (1,)), ((), ())), preferred_element_type=jnp.float32)
        return s if allowed is None else jnp.where(allowed, s, NEG)

    out = []
    s = score(qs[0])
    for i in range(len(qs)):
        following = score(qs[i + 1]) if i + 1 < len(qs) else None
        out.append(softmax_step(s, v, states[i]))
        s = following
    return tuple(out)


def kernel(
    pq_ref, pkv_ref, dest_ref, pool_ref, table_ref, len_ref, dq_ref, dn_ref,
    out_ref, arr_ref, dec_ref,
    kv, qin, obuf, pages, arr_send, pool, dq, dn, qd, dec_send, stat_send, dec_recv, stat_recv, fin, finb,
    local_sem, q_send, q_recv, kv_send, kv_recv, o_send, o_recv, a_send, a_recv,
    d_send, d_recv, s_send, s_recv, f_send, f_recv,
):
    c, g = lax.axis_index("ctx"), lax.axis_index("grp")
    x, y, z, co = c // 4, c % 4, g // 2, g % 2
    py = y // 2
    hy = (y % 2 + py) % 2
    k = x * 2 + hy
    ox = 1 - x
    yx = y + 1 - 2 * (y % 2)
    my = 3 - y
    myx = my + 1 - 2 * (my % 2)
    gm = z * 2 + 1 - co

    c_a, c_b, c_c = x * 4 + yx, ox * 4 + my, ox * 4 + myx
    q_peers = [
        (c_a, g, x * 2 + 1 - hy),
        (c_b, gm, ox * 2 + hy),
        (c_c, gm, ox * 2 + 1 - hy),
    ]
    kv_peers = [
        (c_a, g, x * 2 + 1 - hy),
        (ox * 4 + y, g, ox * 2 + hy),
        (ox * 4 + yx, g, ox * 2 + 1 - hy),
    ]

    def dev(cc, gg):
        return {"ctx": cc, "grp": gg}

    def remote(src, dst, send, recv, cc, gg):
        return pltpu.make_async_remote_copy(
            src_ref=src, dst_ref=dst, send_sem=send, recv_sem=recv, device_id=dev(cc, gg), device_id_type=MESH
        )

    loads = [
        pltpu.make_async_copy(dq_ref, dq, local_sem.at[0]),
        pltpu.make_async_copy(dn_ref, dn, local_sem.at[1]),
        pltpu.make_async_copy(pkv_ref, pages, local_sem.at[2]),
        pltpu.make_async_copy(pool_ref, pool, local_sem.at[3]),
    ]
    own_q = pltpu.make_async_copy(pq_ref.at[:, pl.ds(pl.multiple_of(k * 1024, 1024), 1024)], qin.at[3], local_sem.at[4])
    own_kv = pltpu.make_async_copy(pkv_ref.at[:, pl.ds(pl.multiple_of(k * 256, 256), 256)], kv.at[x, y, g], local_sem.at[5])
    own_kv.start()
    own_q.start()
    for load in loads:
        load.start()

    barrier = pltpu.get_barrier_semaphore()
    partners = [((c + i) % 8, g) for i in range(1, 8)] + [(c, (g + i) % 8) for i in range(1, 8)]
    partners += [(c_b, gm), (c_c, gm)]
    for cc, gg in partners:
        pl.semaphore_signal(barrier, inc=1, device_id=dev(cc, gg), device_id_type=MESH)
    pl.semaphore_wait(barrier, len(partners))

    kv_first = []
    for i, (cc, gg, kk) in enumerate(kv_peers):
        kv_first.append(
            remote(pkv_ref.at[:, pl.ds(pl.multiple_of(kk * 256, 256), 256)], kv.at[x, y, g], kv_send.at[i], kv_recv.at[i], cc, gg)
        )
        kv_first[-1].start()
    q_copies = []
    for i, (cc, gg, kk) in enumerate(q_peers):
        q_copies.append(
            remote(pq_ref.at[:, pl.ds(pl.multiple_of(kk * 1024, 1024), 1024)], qin.at[i], q_send.at[i], q_recv.at[i], cc, gg)
        )
        q_copies[-1].start()

    own_kv.wait()
    for i, (cc, gg, kk) in enumerate(kv_peers):
        here = kv.at[cc // 4, cc % 4, gg]
        remote(here, here, kv_send.at[i], kv_recv.at[i], cc, gg).wait_recv()

    mine = kv.at[:, pl.ds(2 * py, 2), g]
    theirs = kv.at[:, pl.ds(2 - 2 * py, 2), g]
    y_copy = remote(mine, mine, kv_send.at[3], kv_recv.at[3], x * 4 + my, g)
    y_copy.start()
    z_peers = [((z + d) % 4) * 2 + co for d in (1, 3, 2)]
    z_from = [((z + 4 - d) % 4) * 2 + co for d in (1, 3, 2)]
    z_copies = []
    for i, gg in enumerate(z_peers):
        z_copies.append(remote(mine, mine, kv_send.at[4 + i], kv_recv.at[4 + i], c, gg))
        z_copies[-1].start()
    sib = gm

    loads[0].wait()
    for t in range(4):
        for head in range(32):
            row = (head // 4) * 16 + t * 4 + head % 4
            qd[pl.ds(row, 32, stride=128), :] = dq[t, :, head * HD : (head + 1) * HD].astype(jnp.float32)

    remote(theirs, theirs, kv_send.at[3], kv_recv.at[3], x * 4 + my, g).wait_recv()
    for i, gg in enumerate(z_peers):
        z_copies.append(remote(theirs, theirs, kv_send.at[7 + i], kv_recv.at[7 + i], c, gg))
        z_copies[-1].start()
    whole = kv.at[:, :, g]
    sib_copies = [remote(whole, whole, kv_send.at[10], kv_recv.at[10], c, sib)]
    sib_copies[0].start()

    loads[3].wait()
    lane = lax.broadcasted_iota(jnp.int32, (128, 128), 1)

    def request(r, unused):
        kvr = jnp.concatenate([pool[table_ref[r, j]] for j in range(4)], axis=0)
        q = qd[pl.ds(pl.multiple_of(r * 128, 128), 128), :].astype(jnp.bfloat16)
        s = jnp.concatenate(
            [
                lax.dot_general(
                    q[h * 32 : (h + 1) * 32], kvr[:, h * 256 : h * 256 + 128],
                    (((1,), (1,)), ((), ())), preferred_element_type=jnp.float32,
                )
                for h in range(4)
            ],
            axis=0,
        )
        ok = lane + c * 128 < len_ref[r]
        s = jnp.where(ok, s, NEG)
        m = jnp.max(s, axis=1, keepdims=True)
        p = jnp.where(ok, jnp.exp2((s - m) * EXP2), 0.0)
        l = jnp.sum(p, axis=1, keepdims=True)
        pb = p.astype(jnp.bfloat16)
        for h in range(4):
            pv = jnp.dot(
                pb[h * 32 : (h + 1) * 32], kvr[:, h * 256 + 128 : h * 256 + 256], preferred_element_type=jnp.float32
            ).astype(jnp.bfloat16)
            here = pl.ds(pl.multiple_of(r * 16, 16), 16)
            dec_send[2 * h, here, :] = pv[:16]
            dec_send[2 * h + 1, here, :] = pv[16:]
        stat_send[...] = jnp.where(lane == r, m, jnp.where(lane == r + 32, l, stat_send[...]))
        return unused

    stat_send[...] = jnp.zeros_like(stat_send)
    lax.fori_loop(0, 32, request, 0)

    for i, gg in enumerate(z_from):
        for part, base in ((kv.at[:, pl.ds(2 * py, 2), gg], 4), (kv.at[:, pl.ds(2 - 2 * py, 2), gg], 7)):
            remote(part, part, kv_send.at[base + i], kv_recv.at[base + i], c, gg).wait_recv()
        whole = kv.at[:, :, gg]
        sib_copies.append(remote(whole, whole, kv_send.at[11 + i], kv_recv.at[11 + i], c, sib))
        sib_copies[-1].start()

    dec_copies = []
    for i in range(1, 8):
        cc = (c + i) % 8
        dec_copies.append(remote(dec_send.at[cc], dec_recv.at[i], d_send.at[i], d_recv.at[i], cc, g))
        dec_copies.append(
            remote(
                stat_send.at[pl.ds(pl.multiple_of(cc * 16, 16), 16)], stat_recv.at[i], s_send.at[i], s_recv.at[i], cc, g
            )
        )
    for copy in dec_copies:
        copy.start()

    loads[2].wait()
    dests = [dest_ref[p, 0] for p in range(4)]
    ranks = [sum([(dests[q] == dests[p]).astype(jnp.int32) for q in range(p)], jnp.int32(0)) for p in range(4)]
    marks = [dests[p] * 2 + ranks[p] for p in range(4)]

    def slot_page(i, unused):
        page = jnp.zeros((32, 1024), jnp.bfloat16)
        for p in range(4):
            hit = jnp.full((32, 1024), marks[p], jnp.int32) == i
            page = jnp.where(hit, pages[p * 32 : (p + 1) * 32, :], page)
        arr_send[i] = page
        return unused

    lax.fori_loop(0, 16, slot_page, 0)
    arr_copies = []
    for i in range(1, 8):
        gg = (g + i) % 8
        arr_copies.append(
            remote(arr_send.at[pl.ds(2 * gg, 2)], arr_ref.at[pl.ds(2 * g, 2)], a_send.at[i], a_recv.at[i], c, gg)
        )
        arr_copies[-1].start()
    own_arr = pltpu.make_async_copy(arr_send.at[pl.ds(2 * g, 2)], arr_ref.at[pl.ds(2 * g, 2)], local_sem.at[6])
    own_arr.start()

    own_q.wait()
    for i, (cc, gg, kk) in enumerate(q_peers):
        remote(qin.at[i], qin.at[i], q_send.at[i], q_recv.at[i], cc, gg).wait_recv()
    for i, gg in enumerate([sib] + [((z + 4 - d) % 4) * 2 + 1 - co for d in (1, 3, 2)]):
        whole = kv.at[:, :, gg]
        remote(whole, whole, kv_send.at[10 + i], kv_recv.at[10 + i], c, sib).wait_recv()

    row = lax.broadcasted_iota(jnp.int32, (CHAIN, 1024), 0) % 128
    col = lax.broadcasted_iota(jnp.int32, (CHAIN, 1024), 1)
    gap = col - row
    nchain = 1024 // CHAIN
    per = CHAIN // HD

    def prompt_slot(slot, unused):
        cs = jnp.where(slot == 0, c_a, jnp.where(slot == 1, c_b, jnp.where(slot == 2, c_c, c)))
        gs = jnp.where((slot == 1) | (slot == 2), gm, g)
        qs = [
            jnp.concatenate([qin[slot, :, (i * per + j) * HD : (i * per + j + 1) * HD] for j in range(per)], axis=0)
            for i in range(nchain)
        ]

        def chunk(cc):
            both = kv[cc // 4, cc % 4].reshape(1024, 256)
            return both[:, :HD], both[:, HD:]

        def full(cc, states):
            return flash_chunk(qs, *chunk(cc), states, None)

        start = tuple(
            (
                jnp.full((CHAIN, 1), NEG, jnp.float32),
                jnp.zeros((CHAIN, HD), jnp.float32),
                jnp.zeros((CHAIN, HD), jnp.float32),
            )
            for i in range(nchain)
        )
        states = lax.fori_loop(0, cs, full, start)
        states = flash_chunk(qs, *chunk(cs), states, gap <= gs * 128)
        for i in range(nchain):
            m, l, acc = states[i]
            o = (acc / jnp.sum(l, axis=1, keepdims=True)).astype(jnp.bfloat16)
            for j in range(per):
                obuf[slot, :, (i * per + j) * HD : (i * per + j + 1) * HD] = o[j * HD : (j + 1) * HD]
        return unused

    lax.fori_loop(0, 4, prompt_slot, 0)
    columns = pl.ds(pl.multiple_of(k * 1024, 1024), 1024)
    own_out = pltpu.make_async_copy(obuf.at[3], out_ref.at[:, columns], local_sem.at[7])
    own_out.start()
    o_copies = []
    for i, (cc, gg, kk) in enumerate(q_peers):
        o_copies.append(remote(obuf.at[i], out_ref.at[:, columns], o_send.at[i], o_recv.at[i], cc, gg))
        o_copies[-1].start()

    loads[1].wait()
    for i in range(1, 8):
        remote(dec_recv.at[i], dec_recv.at[i], d_send.at[i], d_recv.at[i], c, g).wait_recv()
        remote(stat_recv.at[i], stat_recv.at[i], s_send.at[i], s_recv.at[i], c, g).wait_recv()
    h = c // 2
    q = jnp.concatenate(
        [qd[pl.ds(pl.multiple_of(r * 128 + c * 16, 16), 16), :] for r in range(32)], axis=0
    ).astype(jnp.bfloat16)
    knew = dn[:, :, pl.ds(pl.multiple_of(h * 256, 256), 128)].reshape(128, 128)
    vnew = dn[:, :, pl.ds(pl.multiple_of(h * 256 + 128, 128), 128)].reshape(128, 128)
    s = lax.dot_general(q, knew, (((1,), (1,)), ((), ())), preferred_element_type=jnp.float32)
    drow = lax.broadcasted_iota(jnp.int32, (512, 128), 0)
    dcol = lax.broadcasted_iota(jnp.int32, (512, 128), 1)
    same = dcol % 32 == drow // 16
    ok = same & (dcol // 32 <= (drow % 16) // 4)
    s = jnp.where(ok, s, NEG)
    m_new = jnp.max(s, axis=1, keepdims=True)
    p = jnp.where(ok, jnp.exp2((s - m_new) * EXP2), 0.0)
    l_new = jnp.sum(p, axis=1, keepdims=True)
    o_new = jnp.dot(p.astype(jnp.bfloat16), vnew, preferred_element_type=jnp.float32)

    at_m = dcol == drow // 16
    at_l = dcol == drow // 16 + 32
    new_stat = jnp.sum(
        (jnp.where(at_m, m_new, 0.0) + jnp.where(at_l, l_new, 0.0)).reshape(32, 16, 128), axis=0
    )
    stats = [new_stat, stat_send[pl.ds(pl.multiple_of(c * 16, 16), 16), :]] + [stat_recv[i] for i in range(1, 8)]
    tops = [stat[:, 0:32] for stat in stats]
    sums = [stat[:, 32:64] for stat in stats]
    top = tops[0]
    for other in tops[1:]:
        top = jnp.maximum(top, other)
    fixes = [jnp.exp2((other - top) * EXP2) for other in tops]
    total = fixes[0] * sums[0]
    for fix, part in zip(fixes[1:], sums[1:]):
        total = total + fix * part
    spread = dcol[:, 0:32] == drow[:, 0:32] // 16
    result = None
    for i, fix in enumerate(fixes):
        weight = jnp.sum(
            jnp.where(spread, jnp.concatenate([fix / total] * 32, axis=0), 0.0), axis=1, keepdims=True
        )
        part = o_new if i == 0 else (dec_send[c] if i == 1 else dec_recv[i - 1]).astype(jnp.float32)
        result = part * weight if result is None else result + part * weight
    fin[...] = result
    for t in range(4):
        for j in range(4):
            finb[t, :, j * HD : (j + 1) * HD] = fin[pl.ds(t * 4 + j, 32, stride=16), :].astype(jnp.bfloat16)
    dcols = pl.ds(pl.multiple_of(c * 512, 512), 512)
    own_dec = pltpu.make_async_copy(finb, dec_ref.at[:, :, dcols], local_sem.at[8])
    own_dec.start()
    f_copies = []
    for i in range(1, 8):
        f_copies.append(
            remote(finb, dec_ref.at[:, :, dcols], f_send.at[i], f_recv.at[i], (c + i) % 8, g)
        )
        f_copies[-1].start()

    for i in range(1, 8):
        gg = (g + 8 - i) % 8
        here = arr_ref.at[pl.ds(2 * gg, 2)]
        remote(here, here, a_send.at[i], a_recv.at[i], c, gg).wait_recv()
        cc = (c + 8 - i) % 8
        here = dec_ref.at[:, :, pl.ds(pl.multiple_of(cc * 512, 512), 512)]
        remote(here, here, f_send.at[i], f_recv.at[i], cc, g).wait_recv()
    for i, (cc, gg, kk) in enumerate(q_peers):
        here = out_ref.at[:, pl.ds(pl.multiple_of(kk * 1024, 1024), 1024)]
        remote(here, here, o_send.at[i], o_recv.at[i], cc, gg).wait_recv()
    for copy in kv_first + [y_copy] + z_copies + sib_copies + q_copies + dec_copies + arr_copies + o_copies + f_copies:
        copy.wait_send()
    own_arr.wait()
    own_out.wait()
    own_dec.wait()


def on_device(prefill_query, prefill_kv, page_dest, cache_pool, page_table, context_len, dec_query, dec_new):
    any_spec, smem = pl.BlockSpec(memory_space=pl.ANY), pl.BlockSpec(memory_space=pltpu.SMEM)
    bf16, f32 = jnp.bfloat16, jnp.float32
    dma = pltpu.SemaphoreType.DMA
    out, arrivals, dec = pl.pallas_call(
        kernel,
        out_shape=(
            jax.ShapeDtypeStruct((128, 4096), bf16),
            jax.ShapeDtypeStruct((16, 32, 1024), bf16),
            jax.ShapeDtypeStruct((4, 32, 4096), bf16),
        ),
        in_specs=[any_spec, any_spec, smem, any_spec, smem, smem, any_spec, any_spec],
        out_specs=(any_spec, any_spec, any_spec),
        scratch_shapes=[
            pltpu.VMEM((2, 4, 8, 128, 256), bf16),
            pltpu.VMEM((4, 128, 1024), bf16),
            pltpu.VMEM((4, 128, 1024), bf16),
            pltpu.VMEM((128, 1024), bf16),
            pltpu.VMEM((16, 32, 1024), bf16),
            pltpu.VMEM((128, 32, 1024), bf16),
            pltpu.VMEM((4, 32, 4096), bf16),
            pltpu.VMEM((4, 32, 1024), bf16),
            pltpu.VMEM((32 * 128, 128), f32),
            pltpu.VMEM((8, 512, 128), bf16),
            pltpu.VMEM((128, 128), f32),
            pltpu.VMEM((8, 512, 128), bf16),
            pltpu.VMEM((8, 16, 128), f32),
            pltpu.VMEM((512, 128), f32),
            pltpu.VMEM((4, 32, 512), bf16),
            dma((9,)),
            dma((3,)), dma((3,)), dma((14,)), dma((14,)), dma((3,)), dma((3,)),
            dma((8,)), dma((8,)), dma((8,)), dma((8,)), dma((8,)), dma((8,)), dma((8,)), dma((8,)),
        ],
        compiler_params=pltpu.CompilerParams(
            collective_id=0, has_side_effects=True, vmem_limit_bytes=58 * 2**20
        ),
        cost_estimate=pl.CostEstimate(flops=10**10, bytes_accessed=20 * 2**20, transcendentals=2 * 10**7),
        name="serving_step",
    )(
        prefill_query, prefill_kv, page_dest, cache_pool.reshape(128, 32, 1024), page_table, context_len,
        dec_query, dec_new,
    )
    return out, arrivals.reshape(1, 1, 16, 32, 1024), dec


def solution(mesh):
    placed = (
        P(("ctx", "grp"), "head"),
        P(("ctx", "grp"), "head"),
        P(("ctx", "grp"), None),
        P("ctx", "grp", None, None, "head"),
        P("grp", "ctx"),
        P("grp"),
        P(None, "grp", "head"),
        P(None, "grp", "head"),
    )
    return jax.shard_map(
        on_device,
        mesh=mesh,
        in_specs=placed,
        out_specs=(
            P(("ctx", "grp"), "head"),
            P("grp", "ctx", None, None, "head"),
            P(None, "grp", "head"),
        ),
        check_vma=False,
    )
```

time: 583 us -> 118 us (0.20)
  matrix products: 173 us -> 0 us
  waiting for transfers between devices: 111 us -> 0 us
  Pallas kernels: 0 us -> 106 us
  local copies, waits for them, and re-layouts: 112 us -> 9.54 us
  other arithmetic: 92.8 us -> 0 us
  blocking collectives: 74.8 us -> 0 us
  between operations: 16.5 us -> 0.64 us
    dot_general x37 -> x0, matrix products: 173 us -> none  [the longest x16 82.6 us: one_block(): jnp.einsum('kgij,jkd->kgid', weight, pair[:, :, 1], preferred_element_typ...]
    pallas_call x0 -> x1, Pallas kernels: none -> 106 us  [on_device(): pl.pallas_call(kernel, out_shape=(jax.ShapeDtypeStruct((128, 4096), bf16)...]
    reduce_sum x19 -> x0, other arithmetic: 77.2 us -> none  [the longest x16 74.7 us: one_block(): run_sum = run_sum * fix + jnp.sum(expo, axis=-1)]
    all_gather x2 -> x0, waiting for transfers between devices: 69.5 us -> none  [the longest x1 69.5 us: on_device(): piece = lax.all_gather(prefill_kv, ('ctx', 'grp'), axis=0, tiled=True)]
    psum x1 -> x0, waiting for transfers between devices: 40.7 us -> none  [on_device(): lax.psum((summed * fix[..., None]).astype(jnp.bfloat16), 'ctx')]
    dynamic_slice x48 -> x0, local copies, waits for them, and re-layouts: 38.7 us -> none  [on_device(): carry, unused = lax.scan(advance, carry, (blocks, offsets))]
    pmax x1 -> x0, blocking collectives: 32 us -> none  [on_device(): top_all = lax.pmax(top, 'ctx')]
    psum x1 -> x0, blocking collectives: 26.6 us -> none  [on_device(): lax.psum((total * fix).astype(jnp.bfloat16), 'ctx').astype(jnp.float32)]
  transfers between devices with their start and end apart: 3 -> 0, of which waited for: 2 -> 0; matrix products, arithmetic and copies ran while one was open for 2% -> 0% of each run, Pallas kernels for 0% -> 0%
where the time goes in v1:
time: 118 us; the launch traced here: 117 us
  Pallas kernels  106 us (90%)
  local copies, waits for them, and re-layouts  9.54 us (8%)
    pallas_call x1, Pallas kernels, on_device(): pl.pallas_call(kernel, out_shape=(jax.ShapeDtypeStruct((128, 4096), bf16)...  106 us
    unnamed x5, local copies, waits for them, and re-layouts  9.54 us

profile of v1, /device:TPU:1, one launch (start us, length us, event | category | flops | bytes accessed | tf_op | source)
XLA Modules:
  0.0 116.7 jit_solution(15486898582764040778)
XLA Ops:
  0.6 1.3 %copy.11.dest_ref = s32[4,1]{1,0:T(4,128)} copy(s32[4,1]{0,1:T(1,128)} %param.10) | data formatting | bytes 32 | tf_op args[2]
  1.9 1.4 %copy.12.table_ref = s32[32,4]{1,0:T(8,128)} copy(s32[32,4]{0,1:T(4,128)} %param.12) | data formatting | bytes 1024 | tf_op args[4]
  3.3 106.5 %serving_step.1 = (bf16[128,4096]{1,0:T(8,128)(2,1)}, bf16[16,32,1024]{2,1,0:T(8,128)(2,1)}, bf16[4,32,4096]{2,1,0:T(8,128)(2,1)}) custom-call(bf16[128,4096]{1,0:T(8,128)(2,1)} %pq_ref.1, bf16[128,1024]{1,0:T(8,128)(2,1)} %pkv_ref.1, s32[4,1]{1,0:T(4,128)} %copy.11.dest_ref, bf16[128,32,1024]{2,1,0:T(8,128)(2,1)} %bitcast.3, s32[32,4]{1,0:T(8,128)} %copy.12.table_ref, ...), custom_call_target="tpu_custom_call" | custom-call | flops 10000000000 | bytes 20971520 | tf_op jit(solution)/shard_map/serving_step/pallas_call | solution.py:355
  109.8 2.3 %copy.16 = bf16[128,4096]{1,0:T(8,128)(2,1)} copy(bf16[128,4096]{1,0:T(8,128)(2,1)} %get-tuple-element.12) | data formatting | bytes 2097152
  112.1 2.3 %copy.17 = bf16[1,1,16,32,1024]{4,3,2,1,0:T(8,128)(2,1)} copy(bf16[1,1,16,32,1024]{4,3,2,1,0:T(8,128)(2,1)} %bitcast.2) | data formatting | bytes 2097152
  114.4 2.3 %copy.18 = bf16[4,32,4096]{2,1,0:T(8,128)(2,1)} copy(bf16[4,32,4096]{2,1,0:T(8,128)(2,1)} %get-tuple-element.14) | data formatting | bytes 2097152

commit v2 on v1

v2 whole, which is shorter than its diff:
```python
import jax
import jax.numpy as jnp
from jax import lax
from jax.experimental import pallas as pl
from jax.experimental.pallas import tpu as pltpu
from jax.sharding import PartitionSpec as P

HD = 128
NEG = -1e30
SCALE = HD**-0.5
EXP2 = SCALE * 1.4426950408889634
MESH = pl.DeviceIdType.MESH
CHAIN = 256


def softmax_step(s, v, state):
    m, l, acc = state
    mn = jnp.maximum(m, jnp.max(s, axis=1, keepdims=True))
    al = jnp.exp2((m - mn) * EXP2)
    p = jnp.exp2((s - mn) * EXP2)
    part = p[:, 0:HD]
    for t in range(1, s.shape[1] // HD):
        part = part + p[:, t * HD : (t + 1) * HD]
    acc = acc * al + jnp.dot(p.astype(jnp.bfloat16), v, preferred_element_type=jnp.float32)
    return mn, l * al + part, acc


def flash_chunk(qs, k, v, states, allowed):
    def score(q):
        s = lax.dot_general(q, k, (((1,), (1,)), ((), ())), preferred_element_type=jnp.float32)
        return s if allowed is None else jnp.where(allowed, s, NEG)

    out = []
    s = score(qs[0])
    for i in range(len(qs)):
        following = score(qs[i + 1]) if i + 1 < len(qs) else None
        out.append(softmax_step(s, v, states[i]))
        s = following
    return tuple(out)


def kernel(
    pq_ref, pkv_ref, dest_ref, pool_ref, table_ref, len_ref, dq_ref, dn_ref,
    out_ref, arr_ref, dec_ref,
    kv, qin, obuf, pages, arr_send, pool, dq, dn, qd, dec_send, stat_send, dec_recv, stat_recv, fin, finb,
    st_m, st_l, st_acc,
    local_sem, q_send, q_recv, kv_send, kv_recv, o_send, o_recv, a_send, a_recv,
    d_send, d_recv, s_send, s_recv, f_send, f_recv,
):
    c, g = lax.axis_index("ctx"), lax.axis_index("grp")
    x, y, z, co = c // 4, c % 4, g // 2, g % 2
    py = y // 2
    hy = (y % 2 + py) % 2
    k = x * 2 + hy
    ox = 1 - x
    yx = y + 1 - 2 * (y % 2)
    my = 3 - y
    myx = my + 1 - 2 * (my % 2)
    sib = z * 2 + 1 - co

    c_a, c_b, c_c = x * 4 + yx, ox * 4 + my, ox * 4 + myx
    q_peers = [(c_a, x * 2 + 1 - hy), (c_b, ox * 2 + hy), (c_c, ox * 2 + 1 - hy)]
    kv_peers = [(c_a, x * 2 + 1 - hy), (ox * 4 + y, ox * 2 + hy), (ox * 4 + yx, ox * 2 + 1 - hy)]

    def remote(src, dst, send, recv, cc, gg):
        return pltpu.make_async_remote_copy(
            src_ref=src, dst_ref=dst, send_sem=send, recv_sem=recv,
            device_id={"ctx": cc, "grp": gg}, device_id_type=MESH,
        )

    loads = [
        pltpu.make_async_copy(dq_ref, dq, local_sem.at[0]),
        pltpu.make_async_copy(pool_ref, pool, local_sem.at[3]),
        pltpu.make_async_copy(dn_ref, dn, local_sem.at[1]),
        pltpu.make_async_copy(pkv_ref, pages, local_sem.at[2]),
    ]
    own_q = pltpu.make_async_copy(pq_ref.at[:, pl.ds(pl.multiple_of(k * 1024, 1024), 1024)], qin.at[3], local_sem.at[4])
    own_kv = pltpu.make_async_copy(pkv_ref.at[:, pl.ds(pl.multiple_of(k * 256, 256), 256)], kv.at[x, y, g], local_sem.at[5])
    own_kv.start()
    for load in loads:
        load.start()
    own_q.start()

    barrier = pltpu.get_barrier_semaphore()
    partners = [((c + i) % 8, g) for i in range(1, 8)] + [(c, (g + i) % 8) for i in range(1, 8)]
    for cc, gg in partners:
        pl.semaphore_signal(barrier, inc=1, device_id={"ctx": cc, "grp": gg}, device_id_type=MESH)
    pl.semaphore_wait(barrier, len(partners))

    hops = (1, 3, 2)
    z_peers = [((z + d) % 4) * 2 + co for d in hops]
    z_from = [((z + 4 - d) % 4) * 2 + co for d in hops]
    s_from = [((z + 4 - d) % 4) * 2 + 1 - co for d in hops]
    mirror = x * 4 + my
    own_pieces = [c] + [cc for cc, kk in kv_peers]
    mirror_pieces = [mirror, x * 4 + myx, ox * 4 + my, ox * 4 + myx]
    hop_copies = []

    def piece(cc, gg):
        return kv.at[cc // 4, cc % 4, gg]

    def half(first, gg):
        return kv.at[:, pl.ds(2 * py if first else 2 - 2 * py, 2), gg]

    def send_on(src, at, cc, gg):
        hop_copies.append(remote(src, src, kv_send.at[at], kv_recv.at[at], cc, gg))
        hop_copies[-1].start()

    def arrived(src, at, cc, gg):
        remote(src, src, kv_send.at[at], kv_recv.at[at], cc, gg).wait_recv()

    def pass_on(p):
        here = piece(own_pieces[p], g)
        for i, gg in enumerate(z_peers):
            send_on(here, 7 + 3 * p + i, c, gg)
        send_on(here, 3 + p, mirror, g)
        send_on(here, 19 + p, c, sib)

    kv_first = []
    for i, (cc, kk) in enumerate(kv_peers):
        kv_first.append(
            remote(pkv_ref.at[:, pl.ds(pl.multiple_of(kk * 256, 256), 256)], piece(c, g), kv_send.at[i], kv_recv.at[i], cc, g)
        )
        kv_first[-1].start()
    own_kv.wait()
    pass_on(0)
    q_copies = []
    for i, (cc, kk) in enumerate(q_peers):
        q_copies.append(
            remote(pq_ref.at[:, pl.ds(pl.multiple_of(kk * 1024, 1024), 1024)], qin.at[i], q_send.at[i], q_recv.at[i], cc, g)
        )
        q_copies[-1].start()

    loads[0].wait()
    for t in range(4):
        for head in range(32):
            row = (head // 4) * 16 + t * 4 + head % 4
            qd[pl.ds(row, 32, stride=128), :] = dq[t, :, head * HD : (head + 1) * HD].astype(jnp.float32)

    for p in range(1, 4):
        arrived(piece(own_pieces[p], g), p - 1, own_pieces[p], g)
        pass_on(p)

    loads[1].wait()
    lane = lax.broadcasted_iota(jnp.int32, (128, 128), 1)
    stat_send[...] = jnp.zeros_like(stat_send)
    together = 4

    def requests(n, unused):
        numbers = [n * together + i for i in range(together)]
        kvs, scores = [], []
        for r in numbers:
            kvr = jnp.concatenate([pool[table_ref[j, r]] for j in range(4)], axis=0)
            q = qd[pl.ds(pl.multiple_of(r * 128, 128), 128), :].astype(jnp.bfloat16)
            s = jnp.concatenate(
                [
                    lax.dot_general(
                        q[h * 32 : (h + 1) * 32], kvr[:, h * 256 : h * 256 + 128],
                        (((1,), (1,)), ((), ())), preferred_element_type=jnp.float32,
                    )
                    for h in range(4)
                ],
                axis=0,
            )
            kvs.append(kvr)
            scores.append(s)
        oks = [lane + c * 128 < len_ref[r] for r in numbers]
        scores = [jnp.where(ok, s, NEG) for ok, s in zip(oks, scores)]
        tops = [jnp.max(s, axis=1, keepdims=True) for s in scores]
        expos = [jnp.where(ok, jnp.exp2((s - m) * EXP2), 0.0) for ok, s, m in zip(oks, scores, tops)]
        sums = [jnp.sum(p, axis=1, keepdims=True) for p in expos]
        stat = stat_send[...]
        for r, m, l in zip(numbers, tops, sums):
            stat = jnp.where(lane == r, m, jnp.where(lane == r + 32, l, stat))
        stat_send[...] = stat
        for r, kvr, p in zip(numbers, kvs, expos):
            pb = p.astype(jnp.bfloat16)
            for h in range(4):
                pv = jnp.dot(
                    pb[h * 32 : (h + 1) * 32], kvr[:, h * 256 + 128 : h * 256 + 256], preferred_element_type=jnp.float32
                ).astype(jnp.bfloat16)
                here = pl.ds(pl.multiple_of(r * 16, 16), 16)
                dec_send[2 * h, here, :] = pv[:16]
                dec_send[2 * h + 1, here, :] = pv[16:]
        return unused

    lax.fori_loop(0, 16 // together, requests, 0)
    lax.fori_loop(16 // together, 32 // together, requests, 0)

    dec_copies = []
    for i in range(1, 8):
        cc = (c + i) % 8
        dec_copies.append(remote(dec_send.at[cc], dec_recv.at[i], d_send.at[i], d_recv.at[i], cc, g))
        dec_copies.append(
            remote(
                stat_send.at[pl.ds(pl.multiple_of(cc * 16, 16), 16)], stat_recv.at[i], s_send.at[i], s_recv.at[i], cc, g
            )
        )
    for p in range(4):
        for i, gg in enumerate(z_from):
            here = piece(own_pieces[p], gg)
            arrived(here, 7 + 3 * p + i, c, gg)
            send_on(here, 23 + 3 * p + i, c, sib)
    for p in range(4):
        arrived(piece(mirror_pieces[p], g), 3 + p, mirror, g)
    for i, gg in enumerate(z_peers):
        send_on(half(False, g), 35 + i, c, gg)
    send_on(half(False, g), 38, c, sib)

    for copy in dec_copies:
        copy.start()

    loads[3].wait()
    dests = [dest_ref[0, p] for p in range(4)]
    ranks = [sum([(dests[q] == dests[p]).astype(jnp.int32) for q in range(p)], jnp.int32(0)) for p in range(4)]
    marks = [dests[p] * 2 + ranks[p] for p in range(4)]

    def slot_page(i, unused):
        page = jnp.zeros((32, 1024), jnp.bfloat16)
        for p in range(4):
            hit = jnp.full((32, 1024), marks[p], jnp.int32) == i
            page = jnp.where(hit, pages[p * 32 : (p + 1) * 32, :], page)
        arr_send[i] = page
        return unused

    lax.fori_loop(0, 16, slot_page, 0)

    row = lax.broadcasted_iota(jnp.int32, (CHAIN, 1024), 0) % 128
    col = lax.broadcasted_iota(jnp.int32, (CHAIN, 1024), 1)
    allowed = col - row <= g * 128
    nchain = 1024 // CHAIN
    per = CHAIN // HD
    columns = pl.ds(pl.multiple_of(k * 1024, 1024), 1024)

    def queries_of(slot):
        return [
            jnp.concatenate([qin[slot, :, (i * per + j) * HD : (i * per + j + 1) * HD] for j in range(per)], axis=0)
            for i in range(nchain)
        ]

    def chunk(cc):
        both = kv[cc // 4, cc % 4].reshape(1024, 256)
        return both[:, :HD], both[:, HD:]

    def over(qs, first, cs, states):
        pair = 2 * py if first else 2 - 2 * py
        ids = [(j // 2) * 4 + pair + j % 2 for j in range(4)]
        count = sum([(one < cs).astype(jnp.int32) for one in ids], jnp.int32(0))

        def full(j, held):
            return flash_chunk(qs, *chunk((j // 2) * 4 + pair + j % 2), held, None)

        return lax.fori_loop(0, count, full, states)

    def fresh():
        return tuple(
            (
                jnp.full((CHAIN, 1), NEG, jnp.float32),
                jnp.zeros((CHAIN, HD), jnp.float32),
                jnp.zeros((CHAIN, HD), jnp.float32),
            )
            for i in range(nchain)
        )

    def keep(slot, states):
        for i in range(nchain):
            here = pl.ds(i * CHAIN, CHAIN)
            m, l, acc = states[i]
            st_m[slot, here, :] = jnp.broadcast_to(m, (CHAIN, HD))
            st_l[slot, here, :] = l
            st_acc[slot, here, :] = acc

    def kept(slot):
        states = []
        for i in range(nchain):
            here = pl.ds(i * CHAIN, CHAIN)
            states.append((st_m[slot, here, 0:1], st_l[slot, here, :], st_acc[slot, here, :]))
        return tuple(states)

    def finish(slot, states):
        for i in range(nchain):
            m, l, acc = states[i]
            o = (acc / jnp.sum(l, axis=1, keepdims=True)).astype(jnp.bfloat16)
            for j in range(per):
                obuf[slot, :, (i * per + j) * HD : (i * per + j + 1) * HD] = o[j * HD : (j + 1) * HD]

    def pick(j):
        slot = jnp.where(j == 0, 0, jnp.where(j == 1, 3, jnp.where(j == 2, 2, 1)))
        return slot, jnp.where(j == 0, c_a, jnp.where(j == 1, c, jnp.where(j == 2, c_c, c_b)))

    def masked(qs, cs, wanted, states):
        def last(j, held):
            return flash_chunk(qs, *chunk(cs), held, allowed)

        return lax.fori_loop(0, wanted.astype(jnp.int32), last, states)

    def first_pass(j, unused):
        slot, cs = pick(j)

        @pl.when(j != 1)
        def _():
            remote(qin.at[slot], qin.at[slot], q_send.at[slot], q_recv.at[slot], cs, g).wait_recv()

        qs = queries_of(slot)
        states = over(qs, True, cs, fresh())
        keep(slot, masked(qs, cs, j == 0, states))
        return unused

    def second_pass(n, unused):
        j = (n + 2) % 4
        slot, cs = pick(j)
        qs = queries_of(slot)
        states = over(qs, False, cs, kept(slot))
        finish(slot, masked(qs, cs, j != 0, states))

        @pl.when(j != 1)
        def _():
            remote(obuf.at[slot], out_ref.at[:, columns], o_send.at[slot], o_recv.at[slot], cs, g).start()

        return unused

    own_q.wait()
    for p in range(4):
        arrived(piece(own_pieces[p], sib), 19 + p, c, sib)
        for i, gg in enumerate(s_from):
            arrived(piece(own_pieces[p], gg), 23 + 3 * p + i, c, sib)
    lax.fori_loop(0, 4, first_pass, 0)

    for i, gg in enumerate(z_from):
        arrived(half(False, gg), 35 + i, c, gg)
        send_on(half(False, gg), 39 + i, c, sib)
    arr_copies = []
    for i in range(1, 8):
        gg = (g + i) % 8
        arr_copies.append(
            remote(arr_send.at[pl.ds(2 * gg, 2)], arr_ref.at[pl.ds(2 * g, 2)], a_send.at[i], a_recv.at[i], c, gg)
        )
        arr_copies[-1].start()
    own_arr = pltpu.make_async_copy(arr_send.at[pl.ds(2 * g, 2)], arr_ref.at[pl.ds(2 * g, 2)], local_sem.at[6])
    own_arr.start()

    loads[2].wait()
    for i in range(1, 8):
        remote(dec_recv.at[i], dec_recv.at[i], d_send.at[i], d_recv.at[i], c, g).wait_recv()
        remote(stat_recv.at[i], stat_recv.at[i], s_send.at[i], s_recv.at[i], c, g).wait_recv()
    h = c // 2
    q = jnp.concatenate(
        [qd[pl.ds(pl.multiple_of(r * 128 + c * 16, 16), 16), :] for r in range(32)], axis=0
    ).astype(jnp.bfloat16)
    knew = dn[:, :, pl.ds(pl.multiple_of(h * 256, 256), 128)].reshape(128, 128)
    vnew = dn[:, :, pl.ds(pl.multiple_of(h * 256 + 128, 128), 128)].reshape(128, 128)
    s = lax.dot_general(q, knew, (((1,), (1,)), ((), ())), preferred_element_type=jnp.float32)
    drow = lax.broadcasted_iota(jnp.int32, (512, 128), 0)
    dcol = lax.broadcasted_iota(jnp.int32, (512, 128), 1)
    ok = (dcol % 32 == drow // 16) & (dcol // 32 <= (drow % 16) // 4)
    s = jnp.where(ok, s, NEG)
    m_new = jnp.max(s, axis=1, keepdims=True)
    p = jnp.where(ok, jnp.exp2((s - m_new) * EXP2), 0.0)
    l_new = jnp.sum(p, axis=1, keepdims=True)
    o_new = jnp.dot(p.astype(jnp.bfloat16), vnew, preferred_element_type=jnp.float32)

    new_stat = jnp.sum(
        jnp.where(dcol == drow // 16, m_new, jnp.where(dcol == drow // 16 + 32, l_new, 0.0)).reshape(32, 16, 128), axis=0
    )
    stats = [new_stat, stat_send[pl.ds(pl.multiple_of(c * 16, 16), 16), :]] + [stat_recv[i] for i in range(1, 8)]
    tops = [stat[:, 0:32] for stat in stats]
    sums = [stat[:, 32:64] for stat in stats]
    top = tops[0]
    for other in tops[1:]:
        top = jnp.maximum(top, other)
    fixes = [jnp.exp2((other - top) * EXP2) for other in tops]
    total = fixes[0] * sums[0]
    for fix, part in zip(fixes[1:], sums[1:]):
        total = total + fix * part
    spread = dcol[:, 0:32] == drow[:, 0:32] // 16
    result = None
    for i, fix in enumerate(fixes):
        weight = jnp.sum(
            jnp.where(spread, jnp.concatenate([fix / total] * 32, axis=0), 0.0), axis=1, keepdims=True
        )
        part = o_new if i == 0 else (dec_send[c] if i == 1 else dec_recv[i - 1]).astype(jnp.float32)
        result = part * weight if result is None else result + part * weight
    fin[...] = result
    for t in range(4):
        for j in range(4):
            finb[t, :, j * HD : (j + 1) * HD] = fin[pl.ds(t * 4 + j, 32, stride=16), :].astype(jnp.bfloat16)
    dcols = pl.ds(pl.multiple_of(c * 512, 512), 512)
    own_dec = pltpu.make_async_copy(finb, dec_ref.at[:, :, dcols], local_sem.at[8])
    own_dec.start()
    f_copies = []
    for i in range(1, 8):
        f_copies.append(
            remote(finb, dec_ref.at[:, :, dcols], f_send.at[i], f_recv.at[i], (c + i) % 8, g)
        )
        f_copies[-1].start()

    arrived(half(False, sib), 38, c, sib)
    for i, gg in enumerate(s_from):
        arrived(half(False, gg), 39 + i, c, sib)
    lax.fori_loop(0, 4, second_pass, 0)
    own_out = pltpu.make_async_copy(obuf.at[3], out_ref.at[:, columns], local_sem.at[7])
    own_out.start()

    for i in range(1, 8):
        gg = (g + 8 - i) % 8
        here = arr_ref.at[pl.ds(2 * gg, 2)]
        remote(here, here, a_send.at[i], a_recv.at[i], c, gg).wait_recv()
        cc = (c + 8 - i) % 8
        here = dec_ref.at[:, :, pl.ds(pl.multiple_of(cc * 512, 512), 512)]
        remote(here, here, f_send.at[i], f_recv.at[i], cc, g).wait_recv()
    for i, (cc, kk) in enumerate(q_peers):
        here = out_ref.at[:, pl.ds(pl.multiple_of(kk * 1024, 1024), 1024)]
        remote(obuf.at[i], here, o_send.at[i], o_recv.at[i], cc, g).wait()
    for copy in kv_first + hop_copies + q_copies + dec_copies + arr_copies + f_copies:
        copy.wait_send()
    own_arr.wait()
    own_out.wait()
    own_dec.wait()


def hand_out(out_in, arr_in, dec_in, out_ref, arr_ref, dec_ref, out_buf, arr_buf, dec_buf, sem_in, sem_out):
    moves = []
    for src, buf, dst in ((out_in, out_buf, out_ref), (arr_in, arr_buf, arr_ref), (dec_in, dec_buf, dec_ref)):
        rows = src.shape[0] // 4
        for i in range(4):
            here = pl.ds(i * rows, rows)
            n = len(moves)
            moves.append(
                (
                    pltpu.make_async_copy(src.at[here], buf.at[here], sem_in.at[n]),
                    pltpu.make_async_copy(buf.at[here], dst.at[here], sem_out.at[n]),
                )
            )
    for load, store in moves:
        load.start()
    for load, store in moves:
        load.wait()
        store.start()
    for load, store in moves:
        store.wait()


def on_device(prefill_query, prefill_kv, page_dest, cache_pool, page_table, context_len, dec_query, dec_new):
    any_spec, smem = pl.BlockSpec(memory_space=pl.ANY), pl.BlockSpec(memory_space=pltpu.SMEM)
    bf16, f32 = jnp.bfloat16, jnp.float32
    dma = pltpu.SemaphoreType.DMA
    out, arrivals, dec = pl.pallas_call(
        kernel,
        out_shape=(
            jax.ShapeDtypeStruct((128, 4096), bf16),
            jax.ShapeDtypeStruct((16, 32, 1024), bf16),
            jax.ShapeDtypeStruct((4, 32, 4096), bf16),
        ),
        in_specs=[any_spec, any_spec, smem, any_spec, smem, smem, any_spec, any_spec],
        out_specs=(any_spec, any_spec, any_spec),
        scratch_shapes=[
            pltpu.VMEM((2, 4, 8, 128, 256), bf16),
            pltpu.VMEM((4, 128, 1024), bf16),
            pltpu.VMEM((4, 128, 1024), bf16),
            pltpu.VMEM((128, 1024), bf16),
            pltpu.VMEM((16, 32, 1024), bf16),
            pltpu.VMEM((128, 32, 1024), bf16),
            pltpu.VMEM((4, 32, 4096), bf16),
            pltpu.VMEM((4, 32, 1024), bf16),
            pltpu.VMEM((32 * 128, 128), f32),
            pltpu.VMEM((8, 512, 128), bf16),
            pltpu.VMEM((128, 128), f32),
            pltpu.VMEM((8, 512, 128), bf16),
            pltpu.VMEM((8, 16, 128), f32),
            pltpu.VMEM((512, 128), f32),
            pltpu.VMEM((4, 32, 512), bf16),
            pltpu.VMEM((4, 1024, 128), f32),
            pltpu.VMEM((4, 1024, 128), f32),
            pltpu.VMEM((4, 1024, 128), f32),
            dma((9,)),
            dma((3,)), dma((3,)), dma((42,)), dma((42,)), dma((3,)), dma((3,)),
            dma((8,)), dma((8,)), dma((8,)), dma((8,)), dma((8,)), dma((8,)), dma((8,)), dma((8,)),
        ],
        compiler_params=pltpu.CompilerParams(
            collective_id=0, has_side_effects=True, vmem_limit_bytes=58 * 2**20
        ),
        cost_estimate=pl.CostEstimate(flops=10**10, bytes_accessed=20 * 2**20, transcendentals=2 * 10**7),
        name="serving_step",
    )(
        prefill_query, prefill_kv, page_dest.T, cache_pool.reshape(128, 32, 1024), page_table.T, context_len,
        dec_query, dec_new,
    )
    out, arrivals, dec = pl.pallas_call(
        hand_out,
        out_shape=tuple(jax.ShapeDtypeStruct(a.shape, a.dtype) for a in (out, arrivals, dec)),
        in_specs=[pl.BlockSpec(memory_space=pltpu.HBM)] * 3,
        out_specs=(pl.BlockSpec(memory_space=pltpu.HBM),) * 3,
        scratch_shapes=[pltpu.VMEM(a.shape, a.dtype) for a in (out, arrivals, dec)] + [dma((12,)), dma((12,))],
        cost_estimate=pl.CostEstimate(flops=0, bytes_accessed=6 * 2**20, transcendentals=0),
        name="hand_out",
    )(out, arrivals, dec)
    return out, arrivals.reshape(1, 1, 16, 32, 1024), dec


def solution(mesh):
    placed = (
        P(("ctx", "grp"), "head"),
        P(("ctx", "grp"), "head"),
        P(("ctx", "grp"), None),
        P("ctx", "grp", None, None, "head"),
        P("grp", "ctx"),
        P("grp"),
        P(None, "grp", "head"),
        P(None, "grp", "head"),
    )
    return jax.shard_map(
        on_device,
        mesh=mesh,
        in_specs=placed,
        out_specs=(
            P(("ctx", "grp"), "head"),
            P("grp", "ctx", None, None, "head"),
            P(None, "grp", "head"),
        ),
        check_vma=False,
    )
```

time: 118 us -> 82.1 us (0.70)
  Pallas kernels: 106 us -> 81.3 us
  local copies, waits for them, and re-layouts: 9.54 us -> 0 us
    pallas_call x1, Pallas kernels: 106 us -> 78.5 us  [on_device(): pl.pallas_call(kernel, out_shape=(jax.ShapeDtypeStruct((128, 4096), bf16)...]
    unnamed x5 -> x0, local copies, waits for them, and re-layouts: 9.54 us -> none
    pallas_call x0 -> x1, Pallas kernels: none -> 2.81 us  [on_device(): pl.pallas_call(hand_out, out_shape=tuple((jax.ShapeDtypeStruct(a.shape, a...]
where the time goes in v2:
time: 82.1 us; the launch traced here: 81.9 us
  Pallas kernels  81.3 us (99%)
    pallas_call x1, Pallas kernels, on_device(): pl.pallas_call(kernel, out_shape=(jax.ShapeDtypeStruct((128, 4096), bf16)...  78.5 us
    pallas_call x1, Pallas kernels, on_device(): pl.pallas_call(hand_out, out_shape=tuple((jax.ShapeDtypeStruct(a.shape, a...  2.81 us

profile of v2, /device:TPU:1, one launch (start us, length us, event | category | flops | bytes accessed | tf_op | source)
XLA Modules:
  0.0 81.9 jit_solution(7021687119826885043)
XLA Ops:
  0.6 78.5 %serving_step.1 = (bf16[128,4096]{1,0:T(8,128)(2,1)}, bf16[16,32,1024]{2,1,0:T(8,128)(2,1)}, bf16[4,32,4096]{2,1,0:T(8,128)(2,1)}) custom-call(bf16[128,4096]{1,0:T(8,128)(2,1)} %pq_ref.1, bf16[128,1024]{1,0:T(8,128)(2,1)} %pkv_ref.1, s32[1,4]{1,0:T(1,128)} %bitcast.7, bf16[128,32,1024]{2,1,0:T(8,128)(2,1)} %bitcast.4, s32[4,32]{1,0:T(4,128)} %bitcast.6, ...), custom_call_target="tpu_custom_call" | custom-call | flops 10000000000 | bytes 20971520 | tf_op jit(solution)/shard_map/serving_step/pallas_call | solution.py:447
  79.1 2.8 %hand_out.1 = (bf16[128,4096]{1,0:T(8,128)(2,1)}, bf16[16,32,1024]{2,1,0:T(8,128)(2,1)}, bf16[4,32,4096]{2,1,0:T(8,128)(2,1)}) custom-call(bf16[128,4096]{1,0:T(8,128)(2,1)} %get-tuple-element.9.out_in, bf16[16,32,1024]{2,1,0:T(8,128)(2,1)} %get-tuple-element.10.arr_in, bf16[4,32,4096]{2,1,0:T(8,128)(2,1)} %get-tuple-element.11.dec_in), custom_call_target="tpu_custom_call" | custom-call | bytes 6291456 | tf_op jit(solution)/shard_map/hand_out/pallas_call | solution.py:488

commit v3 on v2

--- a/solution.py
+++ b/solution.py
@@ -26,23 +26,27 @@
 
 
 def flash_chunk(qs, k, v, states, allowed):
+    m_ref, l_ref, acc_ref = states
+
     def score(q):
         s = lax.dot_general(q, k, (((1,), (1,)), ((), ())), preferred_element_type=jnp.float32)
         return s if allowed is None else jnp.where(allowed, s, NEG)
 
-    out = []
     s = score(qs[0])
     for i in range(len(qs)):
         following = score(qs[i + 1]) if i + 1 < len(qs) else None
-        out.append(softmax_step(s, v, states[i]))
+        here = pl.ds(i * CHAIN, CHAIN)
+        m, l, acc = softmax_step(s, v, (m_ref[here, 0:1], l_ref[here, :], acc_ref[here, :]))
+        m_ref[here, :] = jnp.broadcast_to(m, (CHAIN, HD))
+        l_ref[here, :] = l
+        acc_ref[here, :] = acc
         s = following
-    return tuple(out)
 
 
 def kernel(
     pq_ref, pkv_ref, dest_ref, pool_ref, table_ref, len_ref, dq_ref, dn_ref,
     out_ref, arr_ref, dec_ref,
-    kv, qin, obuf, pages, arr_send, pool, dq, dn, qd, dec_send, stat_send, dec_recv, stat_recv, fin, finb,
+    kv, qin, obuf, pages, arr_send, pool, dq, dn, qd, dec_send, stat_send, dec_recv, stat_recv, fin, finb, finx,
     st_m, st_l, st_acc,
     local_sem, q_send, q_recv, kv_send, kv_recv, o_send, o_recv, a_send, a_recv,
     d_send, d_recv, s_send, s_recv, f_send, f_recv,
@@ -187,6 +191,30 @@
     lax.fori_loop(0, 16 // together, requests, 0)
     lax.fori_loop(16 // together, 32 // together, requests, 0)
 
+    loads[2].wait()
+    h = c // 2
+    q = jnp.concatenate(
+        [qd[pl.ds(pl.multiple_of(r * 128 + c * 16, 16), 16), :] for r in range(32)], axis=0
+    ).astype(jnp.bfloat16)
+    knew = dn[:, :, pl.ds(pl.multiple_of(h * 256, 256), 128)].reshape(128, 128)
+    vnew = dn[:, :, pl.ds(pl.multiple_of(h * 256 + 128, 128), 128)].reshape(128, 128)
+    s = lax.dot_general(q, knew, (((1,), (1,)), ((), ())), preferred_element_type=jnp.float32)
+    drow = lax.broadcasted_iota(jnp.int32, (512, 128), 0)
+    dcol = lax.broadcasted_iota(jnp.int32, (512, 128), 1)
+    ok = (dcol % 32 == drow // 16) & (dcol // 32 <= (drow % 16) // 4)
+    s = jnp.where(ok, s, NEG)
+    m_new = jnp.max(s, axis=1, keepdims=True)
+    p = jnp.where(ok, jnp.exp2((s - m_new) * EXP2), 0.0)
+    l_new = jnp.sum(p, axis=1, keepdims=True)
+    fin[...] = jnp.dot(p.astype(jnp.bfloat16), vnew, preferred_element_type=jnp.float32)
+
+    stat_recv[0] = jnp.sum(
+        jnp.where(dcol == drow // 16, m_new, jnp.where(dcol == drow // 16 + 32, l_new, 0.0)).reshape(32, 16, 128), axis=0
+    )
+    st_m[...] = jnp.full_like(st_m, NEG)
+    st_l[...] = jnp.zeros_like(st_l)
+    st_acc[...] = jnp.zeros_like(st_acc)
+
     dec_copies = []
     for i in range(1, 8):
         cc = (c + i) % 8
@@ -242,45 +270,29 @@
         both = kv[cc // 4, cc % 4].reshape(1024, 256)
         return both[:, :HD], both[:, HD:]
 
-    def over(qs, first, cs, states):
+    def states_of(slot):
+        return st_m.at[slot], st_l.at[slot], st_acc.at[slot]
+
+    def over(slot, first, cs, diagonal):
+        qs, states = queries_of(slot), states_of(slot)
         pair = 2 * py if first else 2 - 2 * py
         ids = [(j // 2) * 4 + pair + j % 2 for j in range(4)]
         count = sum([(one < cs).astype(jnp.int32) for one in ids], jnp.int32(0))
 
-        def full(j, held):
-            return flash_chunk(qs, *chunk((j // 2) * 4 + pair + j % 2), held, None)
-
-        return lax.fori_loop(0, count, full, states)
-
-    def fresh():
-        return tuple(
-            (
-                jnp.full((CHAIN, 1), NEG, jnp.float32),
-                jnp.zeros((CHAIN, HD), jnp.float32),
-                jnp.zeros((CHAIN, HD), jnp.float32),
-            )
-            for i in range(nchain)
-        )
-
-    def keep(slot, states):
+        def full(j, unused):
+            flash_chunk(qs, *chunk((j // 2) * 4 + pair + j % 2), states, None)
+            return unused
+
+        lax.fori_loop(0, count, full, 0)
+
+        @pl.when(diagonal)
+        def _():
+            flash_chunk(qs, *chunk(cs), states, allowed)
+
+    def finish(slot):
         for i in range(nchain):
             here = pl.ds(i * CHAIN, CHAIN)
-            m, l, acc = states[i]
-            st_m[slot, here, :] = jnp.broadcast_to(m, (CHAIN, HD))
-            st_l[slot, here, :] = l
-            st_acc[slot, here, :] = acc
-
-    def kept(slot):
-        states = []
-        for i in range(nchain):
-            here = pl.ds(i * CHAIN, CHAIN)
-            states.append((st_m[slot, here, 0:1], st_l[slot, here, :], st_acc[slot, here, :]))
-        return tuple(states)
-
-    def finish(slot, states):
-        for i in range(nchain):
-            m, l, acc = states[i]
-            o = (acc / jnp.sum(l, axis=1, keepdims=True)).astype(jnp.bfloat16)
+            o = (st_acc[slot, here, :] / jnp.sum(st_l[slot, here, :], axis=1, keepdims=True)).astype(jnp.bfloat16)
             for j in range(per):
                 obuf[slot, :, (i * per + j) * HD : (i * per + j + 1) * HD] = o[j * HD : (j + 1) * HD]
 
@@ -288,12 +300,6 @@
         slot = jnp.where(j == 0, 0, jnp.where(j == 1, 3, jnp.where(j == 2, 2, 1)))
         return slot, jnp.where(j == 0, c_a, jnp.where(j == 1, c, jnp.where(j == 2, c_c, c_b)))
 
-    def masked(qs, cs, wanted, states):
-        def last(j, held):
-            return flash_chunk(qs, *chunk(cs), held, allowed)
-
-        return lax.fori_loop(0, wanted.astype(jnp.int32), last, states)
-
     def first_pass(j, unused):
         slot, cs = pick(j)
 
@@ -301,17 +307,14 @@
         def _():
             remote(qin.at[slot], qin.at[slot], q_send.at[slot], q_recv.at[slot], cs, g).wait_recv()
 
-        qs = queries_of(slot)
-        states = over(qs, True, cs, fresh())
-        keep(slot, masked(qs, cs, j == 0, states))
+        over(slot, True, cs, j == 0)
         return unused
 
     def second_pass(n, unused):
         j = (n + 2) % 4
         slot, cs = pick(j)
-        qs = queries_of(slot)
-        states = over(qs, False, cs, kept(slot))
-        finish(slot, masked(qs, cs, j != 0, states))
+        over(slot, False, cs, j != 0)
+        finish(slot)
 
         @pl.when(j != 1)
         def _():
@@ -339,30 +342,10 @@
     own_arr = pltpu.make_async_copy(arr_send.at[pl.ds(2 * g, 2)], arr_ref.at[pl.ds(2 * g, 2)], local_sem.at[6])
     own_arr.start()
 
-    loads[2].wait()
     for i in range(1, 8):
         remote(dec_recv.at[i], dec_recv.at[i], d_send.at[i], d_recv.at[i], c, g).wait_recv()
         remote(stat_recv.at[i], stat_recv.at[i], s_send.at[i], s_recv.at[i], c, g).wait_recv()
-    h = c // 2
-    q = jnp.concatenate(
-        [qd[pl.ds(pl.multiple_of(r * 128 + c * 16, 16), 16), :] for r in range(32)], axis=0
-    ).astype(jnp.bfloat16)
-    knew = dn[:, :, pl.ds(pl.multiple_of(h * 256, 256), 128)].reshape(128, 128)
-    vnew = dn[:, :, pl.ds(pl.multiple_of(h * 256 + 128, 128), 128)].reshape(128, 128)
-    s = lax.dot_general(q, knew, (((1,), (1,)), ((), ())), preferred_element_type=jnp.float32)
-    drow = lax.broadcasted_iota(jnp.int32, (512, 128), 0)
-    dcol = lax.broadcasted_iota(jnp.int32, (512, 128), 1)
-    ok = (dcol % 32 == drow // 16) & (dcol // 32 <= (drow % 16) // 4)
-    s = jnp.where(ok, s, NEG)
-    m_new = jnp.max(s, axis=1, keepdims=True)
-    p = jnp.where(ok, jnp.exp2((s - m_new) * EXP2), 0.0)
-    l_new = jnp.sum(p, axis=1, keepdims=True)
-    o_new = jnp.dot(p.astype(jnp.bfloat16), vnew, preferred_element_type=jnp.float32)
-
-    new_stat = jnp.sum(
-        jnp.where(dcol == drow // 16, m_new, jnp.where(dcol == drow // 16 + 32, l_new, 0.0)).reshape(32, 16, 128), axis=0
-    )
-    stats = [new_stat, stat_send[pl.ds(pl.multiple_of(c * 16, 16), 16), :]] + [stat_recv[i] for i in range(1, 8)]
+    stats = [stat_recv[0], stat_send[pl.ds(pl.multiple_of(c * 16, 16), 16), :]] + [stat_recv[i] for i in range(1, 8)]
     tops = [stat[:, 0:32] for stat in stats]
     sums = [stat[:, 32:64] for stat in stats]
     top = tops[0]
@@ -378,7 +361,7 @@
         weight = jnp.sum(
             jnp.where(spread, jnp.concatenate([fix / total] * 32, axis=0), 0.0), axis=1, keepdims=True
         )
-        part = o_new if i == 0 else (dec_send[c] if i == 1 else dec_recv[i - 1]).astype(jnp.float32)
+        part = fin[...] if i == 0 else (dec_send[c] if i == 1 else dec_recv[i - 1]).astype(jnp.float32)
         result = part * weight if result is None else result + part * weight
     fin[...] = result
     for t in range(4):
@@ -387,16 +370,23 @@
     dcols = pl.ds(pl.multiple_of(c * 512, 512), 512)
     own_dec = pltpu.make_async_copy(finb, dec_ref.at[:, :, dcols], local_sem.at[8])
     own_dec.start()
-    f_copies = []
-    for i in range(1, 8):
-        f_copies.append(
-            remote(finb, dec_ref.at[:, :, dcols], f_send.at[i], f_recv.at[i], (c + i) % 8, g)
-        )
+    across = ox * 4 + y
+    f_copies = [remote(finb, finx, f_send.at[0], f_recv.at[0], across, g)]
+    f_copies[0].start()
+    for d in range(1, 4):
+        f_copies.append(remote(finb, dec_ref.at[:, :, dcols], f_send.at[d], f_recv.at[d], x * 4 + (y + d) % 4, g))
         f_copies[-1].start()
 
     arrived(half(False, sib), 38, c, sib)
     for i, gg in enumerate(s_from):
         arrived(half(False, gg), 39 + i, c, sib)
+    remote(finx, finx, f_send.at[0], f_recv.at[0], across, g).wait_recv()
+    xcols = pl.ds(pl.multiple_of(across * 512, 512), 512)
+    other_dec = pltpu.make_async_copy(finx, dec_ref.at[:, :, xcols], local_sem.at[9])
+    other_dec.start()
+    for d in range(1, 4):
+        f_copies.append(remote(finx, dec_ref.at[:, :, xcols], f_send.at[3 + d], f_recv.at[3 + d], x * 4 + (y + d) % 4, g))
+        f_copies[-1].start()
     lax.fori_loop(0, 4, second_pass, 0)
     own_out = pltpu.make_async_copy(obuf.at[3], out_ref.at[:, columns], local_sem.at[7])
     own_out.start()
@@ -405,9 +395,10 @@
         gg = (g + 8 - i) % 8
         here = arr_ref.at[pl.ds(2 * gg, 2)]
         remote(here, here, a_send.at[i], a_recv.at[i], c, gg).wait_recv()
-        cc = (c + 8 - i) % 8
-        here = dec_ref.at[:, :, pl.ds(pl.multiple_of(cc * 512, 512), 512)]
-        remote(here, here, f_send.at[i], f_recv.at[i], cc, g).wait_recv()
+        if i < 7:
+            cc = (x if i < 4 else ox) * 4 + (y + 8 - (i if i < 4 else i - 3)) % 4
+            here = dec_ref.at[:, :, pl.ds(pl.multiple_of(cc * 512, 512), 512)]
+            remote(here, here, f_send.at[i], f_recv.at[i], cc, g).wait_recv()
     for i, (cc, kk) in enumerate(q_peers):
         here = out_ref.at[:, pl.ds(pl.multiple_of(kk * 1024, 1024), 1024)]
         remote(obuf.at[i], here, o_send.at[i], o_recv.at[i], cc, g).wait()
@@ -416,6 +407,7 @@
     own_arr.wait()
     own_out.wait()
     own_dec.wait()
+    other_dec.wait()
 
 
 def hand_out(out_in, arr_in, dec_in, out_ref, arr_ref, dec_ref, out_buf, arr_buf, dec_buf, sem_in, sem_out):
@@ -469,10 +461,11 @@
             pltpu.VMEM((8, 16, 128), f32),
             pltpu.VMEM((512, 128), f32),
             pltpu.VMEM((4, 32, 512), bf16),
+            pltpu.VMEM((4, 32, 512), bf16),
             pltpu.VMEM((4, 1024, 128), f32),
             pltpu.VMEM((4, 1024, 128), f32),
             pltpu.VMEM((4, 1024, 128), f32),
-            dma((9,)),
+            dma((10,)),
             dma((3,)), dma((3,)), dma((42,)), dma((42,)), dma((3,)), dma((3,)),
             dma((8,)), dma((8,)), dma((8,)), dma((8,)), dma((8,)), dma((8,)), dma((8,)), dma((8,)),
         ],

time: 82.1 us -> 78 us (0.950)
  Pallas kernels: 81.3 us -> 77.2 us
    pallas_call x1, Pallas kernels: 78.5 us -> 74.4 us  [on_device(): pl.pallas_call(kernel, out_shape=(jax.ShapeDtypeStruct((128, 4096), bf16)...]
where the time goes in v3:
time: 78 us; the launch traced here: 77.8 us
  Pallas kernels  77.2 us (99%)
    pallas_call x1, Pallas kernels, on_device(): pl.pallas_call(kernel, out_shape=(jax.ShapeDtypeStruct((128, 4096), bf16)...  74.4 us
    pallas_call x1, Pallas kernels, on_device(): pl.pallas_call(hand_out, out_shape=tuple((jax.ShapeDtypeStruct(a.shape, a...  2.81 us

profile of v3, /device:TPU:1, one launch (start us, length us, event | category | flops | bytes accessed | tf_op | source)
XLA Modules:
  0.0 77.8 jit_solution(5493814428519457338)
XLA Ops:
  0.6 74.4 %serving_step.1 = (bf16[128,4096]{1,0:T(8,128)(2,1)}, bf16[16,32,1024]{2,1,0:T(8,128)(2,1)}, bf16[4,32,4096]{2,1,0:T(8,128)(2,1)}) custom-call(bf16[128,4096]{1,0:T(8,128)(2,1)} %pq_ref.1, bf16[128,1024]{1,0:T(8,128)(2,1)} %pkv_ref.1, s32[1,4]{1,0:T(1,128)} %bitcast.7, bf16[128,32,1024]{2,1,0:T(8,128)(2,1)} %bitcast.4, s32[4,32]{1,0:T(4,128)} %bitcast.6, ...), custom_call_target="tpu_custom_call" | custom-call | flops 10000000000 | bytes 20971520 | tf_op jit(solution)/shard_map/serving_step/pallas_call | solution.py:439
  75.0 2.8 %hand_out.1 = (bf16[128,4096]{1,0:T(8,128)(2,1)}, bf16[16,32,1024]{2,1,0:T(8,128)(2,1)}, bf16[4,32,4096]{2,1,0:T(8,128)(2,1)}) custom-call(bf16[128,4096]{1,0:T(8,128)(2,1)} %get-tuple-element.9.out_in, bf16[16,32,1024]{2,1,0:T(8,128)(2,1)} %get-tuple-element.10.arr_in, bf16[4,32,4096]{2,1,0:T(8,128)(2,1)} %get-tuple-element.11.dec_in), custom_call_target="tpu_custom_call" | custom-call | bytes 6291456 | tf_op jit(solution)/shard_map/hand_out/pallas_call | solution.py:481

commit v4 on v3

--- a/solution.py
+++ b/solution.py
@@ -148,7 +148,7 @@
     loads[1].wait()
     lane = lax.broadcasted_iota(jnp.int32, (128, 128), 1)
     stat_send[...] = jnp.zeros_like(stat_send)
-    together = 4
+    together = 8
 
     def requests(n, unused):
         numbers = [n * together + i for i in range(together)]
@@ -216,7 +216,7 @@
     st_acc[...] = jnp.zeros_like(st_acc)
 
     dec_copies = []
-    for i in range(1, 8):
+    for i in (4, 3, 5, 1, 7, 2, 6):
         cc = (c + i) % 8
         dec_copies.append(remote(dec_send.at[cc], dec_recv.at[i], d_send.at[i], d_recv.at[i], cc, g))
         dec_copies.append(

time: 78 us -> 78 us (level)
  no operation moved by 1% of the time
where the time goes in v4:
time: 78 us; the launch traced here: 77.8 us
  Pallas kernels  77.2 us (99%)
    pallas_call x1, Pallas kernels, on_device(): pl.pallas_call(kernel, out_shape=(jax.ShapeDtypeStruct((128, 4096), bf16)...  74.4 us
    pallas_call x1, Pallas kernels, on_device(): pl.pallas_call(hand_out, out_shape=tuple((jax.ShapeDtypeStruct(a.shape, a...  2.81 us

profile of v4, /device:TPU:1, one launch (start us, length us, event | category | flops | bytes accessed | tf_op | source)
XLA Modules:
  0.0 77.8 jit_solution(15968445585670658694)
XLA Ops:
  0.6 74.4 %serving_step.1 = (bf16[128,4096]{1,0:T(8,128)(2,1)}, bf16[16,32,1024]{2,1,0:T(8,128)(2,1)}, bf16[4,32,4096]{2,1,0:T(8,128)(2,1)}) custom-call(bf16[128,4096]{1,0:T(8,128)(2,1)} %pq_ref.1, bf16[128,1024]{1,0:T(8,128)(2,1)} %pkv_ref.1, s32[1,4]{1,0:T(1,128)} %bitcast.7, bf16[128,32,1024]{2,1,0:T(8,128)(2,1)} %bitcast.4, s32[4,32]{1,0:T(4,128)} %bitcast.6, ...), custom_call_target="tpu_custom_call" | custom-call | flops 10000000000 | bytes 20971520 | tf_op jit(solution)/shard_map/serving_step/pallas_call | solution.py:439
  75.0 2.8 %hand_out.1 = (bf16[128,4096]{1,0:T(8,128)(2,1)}, bf16[16,32,1024]{2,1,0:T(8,128)(2,1)}, bf16[4,32,4096]{2,1,0:T(8,128)(2,1)}) custom-call(bf16[128,4096]{1,0:T(8,128)(2,1)} %get-tuple-element.9.out_in, bf16[16,32,1024]{2,1,0:T(8,128)(2,1)} %get-tuple-element.10.arr_in, bf16[4,32,4096]{2,1,0:T(8,128)(2,1)} %get-tuple-element.11.dec_in), custom_call_target="tpu_custom_call" | custom-call | bytes 6291456 | tf_op jit(solution)/shard_map/hand_out/pallas_call | solution.py:481
